TPU v7x, 32 devices: a whole 2x2x4 slice. The times are simulated.
32 devices in a mesh: prompt: 8 (over z, y), head: 4 (over x, core).
Axes of the slice: x: 2, y: 2, z: 4, core: 2. Of those that a mesh axis runs over, the one named last changes fastest.
Arguments:
- queries: bfloat16 [8, 64, 4, 32, 128], P('prompt', None, None, 'head'), may hold values from -12 to 12
- new_keys: bfloat16 [8, 64, 4, 4, 128], P('prompt', None, None, 'head'), may hold values from -8 to 8
- new_values: bfloat16 [8, 64, 4, 4, 128], P('prompt', None, None, 'head'), may hold values from -6 to 6
- prefix_keys: bfloat16 [8, 4, 4096, 128], P('prompt', 'head'), may hold values from -6 to 6
- prefix_values: bfloat16 [8, 4, 4096, 128], P('prompt', 'head'), may hold values from -6 to 6
- suffix_keys: bfloat16 [8, 64, 4, 64, 128], P('prompt', None, 'head'), may hold values from -8 to 8
- suffix_values: bfloat16 [8, 64, 4, 64, 128], P('prompt', None, 'head'), may hold values from -6 to 6
- suffix_lengths: int32 [8, 64], P('prompt'), may hold values from 1 to 64, as said below
- sample_counts: int32 [8], P('prompt'), may hold values from 8 to 64, as said below
- out_weight: bfloat16 [4096, 8192], P('head', 'prompt'), may hold values from -0.09375 to 0.09375
Outputs:
- projected: bfloat16 [4, 512, 8192], P(None, 'head', 'prompt')
Inputs may be any that keep to these rules, and one draw needn't show every extreme that they name: A sample's suffix holds its first suffix_lengths positions; some sample has 64. `sample_counts`: each count is 8, 16, 32 or 64; the samples of a prompt fill its first slots; some prompt has 64.
All inputs are finite; a program needn't handle non-finite values.
Results may differ from a plain program's by a relative error of at most 0.012.
Values may be sent and summed in bfloat16 or wider, within the bound.
A program may use at most 128 MiB of HBM per device.

v0:
```python
import jax
import jax.numpy as jnp
from jax import lax
from jax.sharding import PartitionSpec as P


def block_attend(query_rows, live_count, key_rows, value_rows, score_scale, per_sample):
    row_total = query_rows.shape[0]
    samples = row_total // per_sample
    block_samples = min(16, samples)
    block_rows = block_samples * per_sample
    start_state = (
        jnp.zeros((row_total, query_rows.shape[1]), jnp.float32),
        jnp.zeros((row_total,), jnp.float32),
        jnp.zeros((row_total,), jnp.float32),
    )

    def advance(block_index, state):
        numerator, row_tops, totals = state
        first_row = block_index * block_rows
        query_block = lax.dynamic_slice_in_dim(query_rows, first_row, block_rows, 0)
        scores = (
            lax.dot_general(
                query_block, key_rows, (((1,), (1,)), ((), ())), preferred_element_type=jnp.float32
            )
            * score_scale
        )
        block_top = jnp.max(scores, axis=1)
        weights = jnp.exp(scores - block_top[:, None])
        block_total = jnp.sum(weights, axis=1)
        block_numer = jnp.dot(
            weights.astype(jnp.bfloat16), value_rows, preferred_element_type=jnp.float32
        )
        numerator = lax.dynamic_update_slice_in_dim(numerator, block_numer, first_row, 0)
        row_tops = lax.dynamic_update_slice_in_dim(row_tops, block_top, first_row, 0)
        totals = lax.dynamic_update_slice_in_dim(totals, block_total, first_row, 0)
        return (numerator, row_tops, totals)

    blocks = (live_count + block_samples - 1) // block_samples
    return lax.fori_loop(0, blocks, advance, start_state)


def per_device(
    queries,
    new_keys,
    new_values,
    prefix_keys,
    prefix_values,
    suffix_keys,
    suffix_values,
    suffix_lengths,
    sample_counts,
    out_weight,
):
    local_q = queries[0]
    slot_count, step_count, group_size, head_dim = local_q.shape
    score_scale = head_dim ** (-0.5)
    per_sample = step_count * group_size
    query_rows = local_q.reshape(slot_count * per_sample, head_dim)
    own_keys = prefix_keys[0, 0]
    own_values = prefix_values[0, 0]
    live_count = sample_counts[0]
    prefix_state = block_attend(
        query_rows, live_count, own_keys, own_values, score_scale, per_sample
    )
    prefix_numer = prefix_state[0].reshape(slot_count, step_count, group_size, head_dim)
    prefix_top = prefix_state[1].reshape(slot_count, step_count, group_size)
    prefix_total = prefix_state[2].reshape(slot_count, step_count, group_size)
    tail_keys = suffix_keys[0, :, 0]
    tail_values = suffix_values[0, :, 0]
    fresh_keys = new_keys[0, :, :, 0]
    fresh_values = new_values[0, :, :, 0]
    tail_ok = (
        lax.broadcasted_iota(jnp.int32, (slot_count, tail_keys.shape[1]), 1)
        < suffix_lengths[0][:, None]
    )
    live_rows = lax.broadcasted_iota(jnp.int32, (slot_count,), 0) < live_count
    attended_list = []
    for step_index in range(step_count):
        step_query = local_q[:, step_index]
        tail_scores = (
            jnp.einsum("sgd,skd->sgk", step_query, tail_keys, preferred_element_type=jnp.float32)
            * score_scale
        )
        tail_scores = jnp.where(tail_ok[:, None, :], tail_scores, -1e30)
        fresh_scores = (
            jnp.einsum("sgd,sjd->sgj", step_query, fresh_keys, preferred_element_type=jnp.float32)
            * score_scale
        )
        fresh_ok = (lax.broadcasted_iota(jnp.int32, (step_count,), 0) <= step_index)[None, None, :]
        fresh_scores = jnp.where(fresh_ok, fresh_scores, -1e30)
        pre_top = prefix_top[:, step_index]
        row_top = jnp.maximum(
            jnp.maximum(pre_top, jnp.max(tail_scores, axis=-1)), jnp.max(fresh_scores, axis=-1)
        )
        tail_weights = jnp.where(
            tail_ok[:, None, :], jnp.exp(tail_scores - row_top[..., None]), 0.0
        )
        fresh_weights = jnp.where(fresh_ok, jnp.exp(fresh_scores - row_top[..., None]), 0.0)
        shrink = jnp.exp(pre_top - row_top)
        numerator = prefix_numer[:, step_index] * shrink[..., None]
        numerator = numerator + jnp.einsum(
            "sgk,skd->sgd",
            tail_weights.astype(jnp.bfloat16),
            tail_values,
            preferred_element_type=jnp.float32,
        )
        numerator = numerator + jnp.einsum(
            "sgj,sjd->sgd",
            fresh_weights.astype(jnp.bfloat16),
            fresh_values,
            preferred_element_type=jnp.float32,
        )
        totals = (
            prefix_total[:, step_index] * shrink
            + jnp.sum(tail_weights, axis=-1)
            + jnp.sum(fresh_weights, axis=-1)
        )
        mixed = numerator / totals[..., None]
        attended = jnp.where(live_rows[:, None, None], mixed, 0.0).astype(jnp.bfloat16)
        attended_list.append(attended.reshape(slot_count, group_size * head_dim))
    stacked = jnp.stack(attended_list, 0)
    partial_out = jnp.dot(
        lax.all_gather(stacked, "prompt", axis=1, tiled=True),
        out_weight,
        preferred_element_type=jnp.float32,
    )
    summed = lax.psum_scatter(
        partial_out.astype(jnp.bfloat16), "head", scatter_dimension=1, tiled=True
    )
    return summed


def solution(mesh):
    return jax.shard_map(
        per_device,
        mesh=mesh,
        in_specs=(
            P("prompt", None, None, "head", None),
            P("prompt", None, None, "head", None),
            P("prompt", None, None, "head", None),
            P("prompt", "head", None, None),
            P("prompt", "head", None, None),
            P("prompt", None, "head", None, None),
            P("prompt", None, "head", None, None),
            P("prompt", None),
            P("prompt"),
            P("head", "prompt"),
        ),
        out_specs=P(None, "head", "prompt"),
        check_vma=False,
    )
```

profile of v0, /device:TPU:0, one launch (start us, length us, event | category | flops | bytes accessed | tf_op | source)
XLA Modules:
  0.0 259.5 jit_solution(7075230528854476135)
XLA Ops:
  9.2 3.4 %fusion.117 = (f32[64,8]{1,0:T(8,128)}, f32[64,8,64]{2,1,0:T(8,128)}) fusion(bf16[1,64,1,64,128]{4,3,2,1,0:T(8,128)(2,1)} %param.17, bf16[64,4,8,128]{3,2,0,1:T(8,128)(2,1)S(1)} %bitcast.160, pred[64,64]{1,0:T(8,128)(4,1)S(1)} %iota_compare_fusion), kind=kOutput, calls=%fused_computation.161 | convolution fusion | flops 8486400 | bytes 1320960 | tf_op jit(solution)/shard_map/sgd,skd->sgk/dot_general | solution.py:82
  12.6 3.2 %fusion.115 = (f32[64,8]{1,0:T(8,128)}, f32[64,8,64]{2,1,0:T(8,128)}) fusion(bf16[1,64,1,64,128]{4,3,2,1,0:T(8,128)(2,1)} %param.17, bf16[64,4,8,128]{3,2,0,1:T(8,128)(2,1)S(1)} %bitcast.161, pred[64,64]{1,0:T(8,128)(4,1)S(1)} %iota_compare_fusion), kind=kOutput, calls=%fused_computation.159 | convolution fusion | flops 8486400 | bytes 1320960 | tf_op jit(solution)/shard_map/sgd,skd->sgk/dot_general | solution.py:82
  16.4 3.2 %fusion.113 = (f32[64,8]{1,0:T(8,128)}, f32[64,8,64]{2,1,0:T(8,128)}) fusion(bf16[1,64,1,64,128]{4,3,2,1,0:T(8,128)(2,1)} %param.17, bf16[64,4,8,128]{3,2,0,1:T(8,128)(2,1)S(1)} %bitcast.162, pred[64,64]{1,0:T(8,128)(4,1)S(1)} %iota_compare_fusion), kind=kOutput, calls=%fused_computation.157 | convolution fusion | flops 8486400 | bytes 1320960 | tf_op jit(solution)/shard_map/sgd,skd->sgk/dot_general | solution.py:82
  20.1 2.6 fusion.111
  24.3 53.7 %while.14 = (s32[]{:T(128)}, f32[2048,128]{1,0:T(8,128)}, f32[2048]{0:T(1024)S(1)}, f32[2048]{0:T(1024)S(1)}, s32[]{:T(128)}, /*index=5*/bf16[2048,128]{1,0:T(8,...) while((s32[]{:T(128)}, f32[2048,128]{1,0:T(8,128)}, ...), condition=%wide.region_3.4_spmd, body=%wide.region_0.3_spmd.sunk | while | flops 1090518016 | bytes 65421548 | solution.py:40
  24.3 2.7 %multiply_reduce_fusion.2 = (f32[512]{0:T(512)S(1)}, f32[512,4096]{1,0:T(8,128)S(1)}) fusion(bf16[4096,128]{1,0:T(8,128)(2,1)} %get-tuple-element.195, bf16[2048,128]{1,0:T(8,128)(2,1)} %get-tuple-element.194, s32[]{:T(128)S(6)} %select_n.164), kind=kOutput, calls=%fused_computation.1.clone.1 | convolution fusion | flops 541064704 | bytes 9570308 | tf_op jit(solution)/shard_map/while/body/dot_general | solution.py:23
  27.0 3.2 %copy-done.1 = f32[512,4096]{1,0:T(8,128)} copy-done((f32[512,4096]{1,0:T(8,128)}, f32[512,4096]{1,0:T(8,128)S(1)}, u32[]{:S(2)}) %copy-start.1) | copy-done | bytes 8388632 | tf_op jit(solution)/shard_map/while
  32.0 5.5 %fusion.129 = f32[2048,128]{1,0:T(8,128)} fusion(f32[2048,128]{1,0:T(8,128)} %get-tuple-element.178, s32[]{:T(128)S(6)} %select_n.164, bf16[4096,128]{1,0:T(8,128)(2,1)S(1)} %copy-done.2, f32[512,4096]{1,0:T(8,128)} %copy-done.1, f32[512]{0:T(512)S(1)} %get-tuple-element.164), kind=kOutput, calls=%fused_computation.5.clone.1 | convolution fusion | flops 543162368 | bytes 9701380 | tf_op jit(solution)/shard_map/while/body/dot_general | solution.py:31
  37.7 2.7 %multiply_reduce_fusion.2 = (f32[512]{0:T(512)S(1)}, f32[512,4096]{1,0:T(8,128)S(1)}) fusion(bf16[4096,128]{1,0:T(8,128)(2,1)} %get-tuple-element.195, bf16[2048,128]{1,0:T(8,128)(2,1)} %get-tuple-element.194, s32[]{:T(128)S(6)} %select_n.164), kind=kOutput, calls=%fused_computation.1.clone.1 | convolution fusion | flops 541064704 | bytes 9570308 | tf_op jit(solution)/shard_map/while/body/dot_general | solution.py:23
  40.4 3.2 %copy-done.1 = f32[512,4096]{1,0:T(8,128)} copy-done((f32[512,4096]{1,0:T(8,128)}, f32[512,4096]{1,0:T(8,128)S(1)}, u32[]{:S(2)}) %copy-start.1) | copy-done | bytes 8388632 | tf_op jit(solution)/shard_map/while
  45.4 5.5 %fusion.129 = f32[2048,128]{1,0:T(8,128)} fusion(f32[2048,128]{1,0:T(8,128)} %get-tuple-element.178, s32[]{:T(128)S(6)} %select_n.164, bf16[4096,128]{1,0:T(8,128)(2,1)S(1)} %copy-done.2, f32[512,4096]{1,0:T(8,128)} %copy-done.1, f32[512]{0:T(512)S(1)} %get-tuple-element.164), kind=kOutput, calls=%fused_computation.5.clone.1 | convolution fusion | flops 543162368 | bytes 9701380 | tf_op jit(solution)/shard_map/while/body/dot_general | solution.py:31
  51.1 2.7 %multiply_reduce_fusion.2 = (f32[512]{0:T(512)S(1)}, f32[512,4096]{1,0:T(8,128)S(1)}) fusion(bf16[4096,128]{1,0:T(8,128)(2,1)} %get-tuple-element.195, bf16[2048,128]{1,0:T(8,128)(2,1)} %get-tuple-element.194, s32[]{:T(128)S(6)} %select_n.164), kind=kOutput, calls=%fused_computation.1.clone.1 | convolution fusion | flops 541064704 | bytes 9570308 | tf_op jit(solution)/shard_map/while/body/dot_general | solution.py:23
  53.8 3.2 %copy-done.1 = f32[512,4096]{1,0:T(8,128)} copy-done((f32[512,4096]{1,0:T(8,128)}, f32[512,4096]{1,0:T(8,128)S(1)}, u32[]{:S(2)}) %copy-start.1) | copy-done | bytes 8388632 | tf_op jit(solution)/shard_map/while
  58.8 5.5 %fusion.129 = f32[2048,128]{1,0:T(8,128)} fusion(f32[2048,128]{1,0:T(8,128)} %get-tuple-element.178, s32[]{:T(128)S(6)} %select_n.164, bf16[4096,128]{1,0:T(8,128)(2,1)S(1)} %copy-done.2, f32[512,4096]{1,0:T(8,128)} %copy-done.1, f32[512]{0:T(512)S(1)} %get-tuple-element.164), kind=kOutput, calls=%fused_computation.5.clone.1 | convolution fusion | flops 543162368 | bytes 9701380 | tf_op jit(solution)/shard_map/while/body/dot_general | solution.py:31
  64.5 2.7 %multiply_reduce_fusion.2 = (f32[512]{0:T(512)S(1)}, f32[512,4096]{1,0:T(8,128)S(1)}) fusion(bf16[4096,128]{1,0:T(8,128)(2,1)} %get-tuple-element.195, bf16[2048,128]{1,0:T(8,128)(2,1)} %get-tuple-element.194, s32[]{:T(128)S(6)} %select_n.164), kind=kOutput, calls=%fused_computation.1.clone.1 | convolution fusion | flops 541064704 | bytes 9570308 | tf_op jit(solution)/shard_map/while/body/dot_general | solution.py:23
  67.2 3.2 %copy-done.1 = f32[512,4096]{1,0:T(8,128)} copy-done((f32[512,4096]{1,0:T(8,128)}, f32[512,4096]{1,0:T(8,128)S(1)}, u32[]{:S(2)}) %copy-start.1) | copy-done | bytes 8388632 | tf_op jit(solution)/shard_map/while
  72.2 5.5 %fusion.129 = f32[2048,128]{1,0:T(8,128)} fusion(f32[2048,128]{1,0:T(8,128)} %get-tuple-element.178, s32[]{:T(128)S(6)} %select_n.164, bf16[4096,128]{1,0:T(8,128)(2,1)S(1)} %copy-done.2, f32[512,4096]{1,0:T(8,128)} %copy-done.1, f32[512]{0:T(512)S(1)} %get-tuple-element.164), kind=kOutput, calls=%fused_computation.5.clone.1 | convolution fusion | flops 543162368 | bytes 9701380 | tf_op jit(solution)/shard_map/while/body/dot_general | solution.py:31
  83.3 2.4 fusion.114
  85.7 2.4 fusion.112
  88.2 2.4 fusion.110
  97.5 2.4 fusion.44
  125.2 76.2 %all-gather.2.cloned.1.call-done = bf16[4,512,1024]{2,1,0:T(8,128)(2,1)} async-done(((bf16[4,64,1024]{2,1,0:T(8,128)(2,1)}), bf16[4,512,1024]{2,1,0:T(8,128)(2,1)}) %all-gather.2.cloned.1.call-update) | async-done | bytes 4194320 | tf_op jit(solution)/shard_map/all_gather | solution.py:124
  201.4 8.3 %convolution_convert_fusion = bf16[4,512,1024]{2,1,0:T(8,128)(2,1)} fusion(bf16[4,512,1024]{2,1,0:T(8,128)(2,1)} %all-gather.2.cloned.1.call-done, bf16[1024,1024]{1,0:T(8,128)(2,1)S(1)} %copy-done), kind=kOutput, calls=%fused_computation.10 | convolution fusion | flops 4297064448 | bytes 10485760 | tf_op jit(solution)/shard_map/dot_general | solution.py:123
  209.7 42.9 %reduce-scatter.2.cloned.1.call-done = bf16[4,128,1024]{2,1,0:T(8,128)(2,1)} async-done(((bf16[4,512,1024]{2,1,0:T(8,128)(2,1)}), bf16[4,128,1024]{2,1,0:T(8,128)(2,1)}) %reduce-scatter.2.cloned.1.call-update) | async-done | bytes 1048592 | tf_op jit(solution)/shard_map/reduce_scatter | solution.py:128
  (82 shorter events, 49.7 us)
Async XLA Ops:
  6.5 194.9 %copy-start = (bf16[1024,1024]{1,0:T(8,128)(2,1)S(1)}, bf16[1024,1024]{1,0:T(8,128)(2,1)}, u32[]{:S(2)}) copy-start(bf16[1024,1024]{1,0:T(8,128)(2,1)} %param.21) | copy-start | bytes 6291460
  6.5 194.8 %all-gather.2.cloned.1.call-start = ((), (), s32[]{:S(2)}) async-start(), calls=%async_computation.1 | async-start | bytes 4718592 | tf_op jit(solution)/shard_map/all_gather | solution.py:124
  9.2 10.9 %copy-start.4 = (bf16[1,64,4,8,128]{4,3,1,2,0:T(8,128)(2,1)}, bf16[1,64,4,8,128]{4,3,1,2,0:T(8,128)(2,1)S(1)}, u32[]{:S(2)}) copy-start(bf16[1,64,4,8,128]{4,3,1,2,0:T(8,128)(2,1)S(1)} %copy.30) | copy-start | bytes 1572868
  24.3 7.7 %copy-start.2 = (bf16[4096,128]{1,0:T(8,128)(2,1)S(1)}, bf16[4096,128]{1,0:T(8,128)(2,1)}, u32[]{:S(2)}) copy-start(bf16[4096,128]{1,0:T(8,128)(2,1)} %get-tuple-element.196) | copy-start | bytes 3145732 | tf_op jit(solution)/shard_map/while
  27.0 3.2 %copy-start.1 = (f32[512,4096]{1,0:T(8,128)}, f32[512,4096]{1,0:T(8,128)S(1)}, u32[]{:S(2)}) copy-start(f32[512,4096]{1,0:T(8,128)S(1)} %get-tuple-element.163) | copy-start | bytes 25165828 | tf_op jit(solution)/shard_map/while
  37.7 7.7 %copy-start.2 = (bf16[4096,128]{1,0:T(8,128)(2,1)S(1)}, bf16[4096,128]{1,0:T(8,128)(2,1)}, u32[]{:S(2)}) copy-start(bf16[4096,128]{1,0:T(8,128)(2,1)} %get-tuple-element.196) | copy-start | bytes 3145732 | tf_op jit(solution)/shard_map/while
  40.4 3.2 %copy-start.1 = (f32[512,4096]{1,0:T(8,128)}, f32[512,4096]{1,0:T(8,128)S(1)}, u32[]{:S(2)}) copy-start(f32[512,4096]{1,0:T(8,128)S(1)} %get-tuple-element.163) | copy-start | bytes 25165828 | tf_op jit(solution)/shard_map/while
  51.1 7.7 %copy-start.2 = (bf16[4096,128]{1,0:T(8,128)(2,1)S(1)}, bf16[4096,128]{1,0:T(8,128)(2,1)}, u32[]{:S(2)}) copy-start(bf16[4096,128]{1,0:T(8,128)(2,1)} %get-tuple-element.196) | copy-start | bytes 3145732 | tf_op jit(solution)/shard_map/while
  53.8 3.2 %copy-start.1 = (f32[512,4096]{1,0:T(8,128)}, f32[512,4096]{1,0:T(8,128)S(1)}, u32[]{:S(2)}) copy-start(f32[512,4096]{1,0:T(8,128)S(1)} %get-tuple-element.163) | copy-start | bytes 25165828 | tf_op jit(solution)/shard_map/while
  64.5 7.7 %copy-start.2 = (bf16[4096,128]{1,0:T(8,128)(2,1)S(1)}, bf16[4096,128]{1,0:T(8,128)(2,1)}, u32[]{:S(2)}) copy-start(bf16[4096,128]{1,0:T(8,128)(2,1)} %get-tuple-element.196) | copy-start | bytes 3145732 | tf_op jit(solution)/shard_map/while
  67.2 3.2 %copy-start.1 = (f32[512,4096]{1,0:T(8,128)}, f32[512,4096]{1,0:T(8,128)S(1)}, u32[]{:S(2)}) copy-start(f32[512,4096]{1,0:T(8,128)S(1)} %get-tuple-element.163) | copy-start | bytes 25165828 | tf_op jit(solution)/shard_map/while
  78.0 0.6 copy-start.6
  78.6 0.6 copy-start.7
  79.2 27.5 %copy-start.3 = (bf16[1,64,1,64,128]{4,3,2,1,0:T(8,128)(2,1)S(1)}, bf16[1,64,1,64,128]{4,3,2,1,0:T(8,128)(2,1)}, u32[]{:S(2)}) copy-start(bf16[1,64,1,64,128]{4,3,2,1,0:T(8,128)(2,1)} %param.18) | copy-start | bytes 3145732
  79.2 33.6 %copy-start.8 = (pred[4]{0:T(512)(128)(4,1)S(1)}, pred[4]{0:T(512)(128)(4,1)}, u32[]{:S(2)}) copy-start(pred[4]{0:T(512)(128)(4,1)} %iota_compare_fusion.1) | copy-start | bytes 16
  92.2 21.7 %copy-start.5 = (f32[64,1,8]{2,1,0:T(1,128)S(1)}, f32[64,1,8]{2,1,0:T(1,128)}, u32[]{:S(2)}) copy-start(f32[64,1,8]{2,1,0:T(1,128)} %get-tuple-element.87) | copy-start | bytes 6148
  92.2 10.9 %copy-start.9 = (pred[64]{0:T(512)(128)(4,1)}, pred[64]{0:T(512)(128)(4,1)S(1)}, u32[]{:S(2)}) copy-start(pred[64]{0:T(512)(128)(4,1)S(1)} %iota_compare_fusion.5) | copy-start | bytes 196
  125.2 127.5 %reduce-scatter.2.cloned.1.call-start = ((), (), s32[]{:S(2)}) async-start(), calls=%async_computation.2 | async-start | bytes 5242880 | tf_op jit(solution)/shard_map/reduce_scatter | solution.py:128
Sparse Core Ops, SparseCore 0:
  125.3 76.0 all-gather.1
  209.9 42.7 reduce-scatter.1
where the time goes:
time: 260 us
  waiting for transfers between devices  119 us (46%)
  matrix products  76.6 us (29%)
  local copies, waits for them, and re-layouts  26.2 us (10%)
  other arithmetic  23 us (9%)
  between operations  14.3 us (6%)
    all_gather x1, waiting for transfers between devices, per_device(): lax.all_gather(stacked, 'prompt', axis=1, tiled=True)  76.2 us
    reduce_scatter x1, waiting for transfers between devices, per_device(): lax.psum_scatter(partial_out.astype(jnp.bfloat16), 'head', scatter_dimens...  42.9 us
    dot_general x4, matrix products, advance(): jnp.dot(weights.astype(jnp.bfloat16), value_rows, preferred_element_type=...  22.1 us
    while x16, local copies, waits for them, and re-layouts  12.9 us
    dot_general x4, matrix products, per_device(): jnp.einsum('sgd,skd->sgk', step_query, tail_keys, preferred_element_type=...  12.4 us
    dot_general x4, matrix products, advance(): lax.dot_general(query_block, key_rows, (((1,), (1,)), ((), ())), preferre...  10.8 us
    dot_general x4, matrix products, per_device(): jnp.einsum('sgd,sjd->sgj', step_query, fresh_keys, preferred_element_type...  9.7 us
    dot_general x1, matrix products, per_device(): jnp.dot(lax.all_gather(stacked, 'prompt', axis=1, tiled=True), out_weight...  8.34 us
  transfers between devices with their start and end apart: 2, of which 2 were waited for; matrix products, arithmetic and copies ran while one was open for 0% of the time, Pallas kernels for 0%

commit v1 on v0

v1 whole, which is shorter than its diff:
```python
import functools
import math

import jax
import jax.numpy as jnp
from jax import lax
from jax.experimental import pallas as pl
from jax.experimental.pallas import tpu as pltpu
from jax.sharding import PartitionSpec as P

NEG = -1e30
SAMPLES = 16
GROUPED = 4


def attend_chunk(
    first, q_ref, key_ref, val_ref, tk_ref, tv_ref, nk_ref, nv_ref, bias_ref, live_ref,
    score_ref, mixed_ref, steps, group,
):
    hd = q_ref.shape[1]
    per = steps * group
    rows = SAMPLES * per
    suffix = tk_ref.shape[0] * per // q_ref.shape[0]
    scale = (hd ** -0.5) * math.log2(math.e)
    nt = (((1,), (1,)), ((), ()))
    f32 = jnp.float32
    prefix = key_ref.shape[0]
    tile = 512
    sub = GROUPED * per
    q = q_ref[pl.ds(pl.multiple_of(first * per, rows), rows), :]
    top = None
    for k in range(prefix // tile):
        s = lax.dot_general(q, key_ref[k * tile:(k + 1) * tile, :], nt, preferred_element_type=f32)
        score_ref[:, k * tile:(k + 1) * tile] = s
        for c in range(tile // 128):
            piece = s[:, c * 128:(c + 1) * 128]
            top = piece if top is None else jnp.maximum(top, piece)
    row_top = jnp.max(top, axis=1, keepdims=True)
    nk = nk_ref[pl.ds(pl.multiple_of(first * steps, SAMPLES * steps), SAMPLES * steps), :]
    nv = nv_ref[pl.ds(pl.multiple_of(first * steps, SAMPLES * steps), SAMPLES * steps), :]
    ns = lax.dot_general(q, nk, nt, preferred_element_type=f32)
    r = lax.broadcasted_iota(jnp.int32, ns.shape, 0)
    j = lax.broadcasted_iota(jnp.int32, ns.shape, 1)
    ok = (j // steps == r // per) & (j % steps <= (r % per) // group)
    ns = jnp.where(ok, ns, NEG)
    row_top = jnp.maximum(row_top, jnp.max(ns, axis=1, keepdims=True))
    width = GROUPED * suffix
    tails = []
    for g in range(SAMPLES // GROUPED):
        at = pl.multiple_of((first + g * GROUPED) * suffix, width)
        ts = lax.dot_general(q[g * sub:(g + 1) * sub], tk_ref[pl.ds(at, width), :], nt, preferred_element_type=f32)
        r = lax.broadcasted_iota(jnp.int32, ts.shape, 0)
        j = lax.broadcasted_iota(jnp.int32, ts.shape, 1)
        ts = jnp.where(j // suffix == r // per, ts + bias_ref[:, pl.ds(at, width)], NEG)
        tails.append(ts)
    tail = jnp.concatenate(tails, axis=0)
    row_top = jnp.maximum(row_top, jnp.max(tail, axis=1, keepdims=True))
    nw = jnp.exp2((ns - row_top) * scale)
    tw = jnp.exp2((tail - row_top) * scale)
    total = jnp.sum(nw, axis=1, keepdims=True) + jnp.sum(tw, axis=1, keepdims=True)
    numer = jnp.dot(nw.astype(jnp.bfloat16), nv, preferred_element_type=f32)
    tw = tw.astype(jnp.bfloat16)
    parts = []
    for g in range(SAMPLES // GROUPED):
        at = pl.multiple_of((first + g * GROUPED) * suffix, width)
        parts.append(jnp.dot(tw[g * sub:(g + 1) * sub], tv_ref[pl.ds(at, width), :], preferred_element_type=f32))
    numer = numer + jnp.concatenate(parts, axis=0)
    wide = None
    for k in range(prefix // tile):
        w = jnp.exp2((score_ref[:, k * tile:(k + 1) * tile] - row_top) * scale).astype(jnp.bfloat16)
        d = jnp.dot(w, val_ref[k * tile:(k + 1) * tile, :], preferred_element_type=f32)
        wide = d if wide is None else wide + d
    numer = numer + wide[:, :hd]
    total = total + wide[:, hd:hd + 1]
    mixed = numer / total
    live = live_ref[pl.ds(pl.multiple_of(first * per, rows), rows), :]
    mixed_ref[...] = jnp.where(live > 0.0, mixed, 0.0)


def place_chunk(mixed_ref, out_ref, row, first, steps, group, hd):
    for t in range(steps):
        for g in range(group):
            piece = mixed_ref[pl.ds(t * group + g, SAMPLES, stride=steps * group), :]
            out_ref[row + t, pl.ds(pl.multiple_of(first, SAMPLES), SAMPLES), g * hd:(g + 1) * hd] = piece.astype(jnp.bfloat16)


def widen(v_ref, val_ref):
    hd = v_ref.shape[1]
    val_ref[:, :hd] = v_ref[...]
    val_ref[:, hd:] = jnp.ones((v_ref.shape[0], hd), val_ref.dtype)


def attention_kernel(
    steps, group, q_ref, k_ref, v_ref, tk_ref, tv_ref, nk_ref, nv_ref, bias_ref, live_ref, out_ref,
    val_ref, score_ref, mixed_ref,
):
    hd = q_ref.shape[1]
    slots = q_ref.shape[0] // (steps * group)
    widen(v_ref, val_ref)

    def body(c, _):
        first = c * SAMPLES
        attend_chunk(first, q_ref, k_ref, val_ref, tk_ref, tv_ref, nk_ref, nv_ref, bias_ref, live_ref,
                     score_ref, mixed_ref, steps, group)
        place_chunk(mixed_ref, out_ref, 0, first, steps, group, hd)
        return 0

    lax.fori_loop(0, slots // SAMPLES, body, 0)


def prepare(queries, new_keys, new_values, prefix_keys, prefix_values, suffix_keys, suffix_values, suffix_lengths, sample_counts):
    _, slots, steps, group, hd = queries.shape
    suffix = suffix_keys.shape[3]
    bias = jnp.where(lax.broadcasted_iota(jnp.int32, (slots, suffix), 1) < suffix_lengths[0][:, None], 0.0, NEG)
    bias = bias.astype(jnp.float32).reshape(1, slots * suffix)
    per = steps * group
    live = (lax.broadcasted_iota(jnp.int32, (slots * per, hd), 0) // per < sample_counts[0]).astype(jnp.float32)
    return (
        queries.reshape(slots * per, hd),
        prefix_keys[0, 0], prefix_values[0, 0],
        suffix_keys.reshape(slots * suffix, hd), suffix_values.reshape(slots * suffix, hd),
        new_keys.reshape(slots * steps, hd), new_values.reshape(slots * steps, hd),
        bias, live,
    )


def per_device(
    queries, new_keys, new_values, prefix_keys, prefix_values, suffix_keys, suffix_values,
    suffix_lengths, sample_counts, out_weight,
):
    _, slots, steps, group, hd = queries.shape
    ins = prepare(queries, new_keys, new_values, prefix_keys, prefix_values, suffix_keys, suffix_values, suffix_lengths, sample_counts)
    prefix = prefix_keys.shape[2]
    stacked = pl.pallas_call(
        functools.partial(attention_kernel, steps, group),
        out_shape=jax.ShapeDtypeStruct((steps, slots, group * hd), jnp.bfloat16),
        in_specs=[pl.BlockSpec(memory_space=pltpu.VMEM)] * 9,
        out_specs=pl.BlockSpec(memory_space=pltpu.VMEM),
        scratch_shapes=[
            pltpu.VMEM((prefix, 2 * hd), jnp.bfloat16),
            pltpu.VMEM((SAMPLES * steps * group, prefix), jnp.float32),
            pltpu.VMEM((SAMPLES * steps * group, hd), jnp.float32),
        ],
        compiler_params=pltpu.CompilerParams(vmem_limit_bytes=48 * 2**20),
    )(*ins)
    partial_out = jnp.dot(
        lax.all_gather(stacked, "prompt", axis=1, tiled=True), out_weight, preferred_element_type=jnp.float32
    )
    return lax.psum_scatter(partial_out.astype(jnp.bfloat16), "head", scatter_dimension=1, tiled=True)


def solution(mesh):
    return jax.shard_map(
        per_device,
        mesh=mesh,
        in_specs=(
            P("prompt", None, None, "head", None),
            P("prompt", None, None, "head", None),
            P("prompt", None, None, "head", None),
            P("prompt", "head", None, None),
            P("prompt", "head", None, None),
            P("prompt", None, "head", None, None),
            P("prompt", None, "head", None, None),
            P("prompt", None),
            P("prompt"),
            P("head", "prompt"),
        ),
        out_specs=P(None, "head", "prompt"),
        check_vma=False,
    )
```

time: 260 us -> 180 us (0.69)
  matrix products: 76.6 us -> 8.33 us
  Pallas kernels: 0 us -> 26.6 us
  other arithmetic: 23 us -> 3.41 us
  local copies, waits for them, and re-layouts: 26.2 us -> 7.71 us
    dot_general x24 -> x0, matrix products: 68.3 us -> none  [the longest x4 22.1 us: advance(): jnp.dot(weights.astype(jnp.bfloat16), value_rows, preferred_element_type=...]
    pallas_call x0 -> x1, Pallas kernels: none -> 26.6 us  [per_device(): pl.pallas_call(functools.partial(attention_kernel, steps, group), out_sha...]
    while x16 -> x0, local copies, waits for them, and re-layouts: 12.9 us -> none
    reduce_sum x9 -> x0, other arithmetic: 12.6 us -> none  [the longest x4 6 us: advance(): block_total = jnp.sum(weights, axis=1)]
    unnamed x17 -> x16, local copies, waits for them, and re-layouts: 2.34 us -> 7.62 us
    another operation x6 -> x0, local copies, waits for them, and re-layouts: 4.9 us -> none  [the longest x4 4.89 us: per_device(): stacked = jnp.stack(attended_list, 0)]
    max x4 -> x0, other arithmetic: 3.2 us -> none  [per_device(): jnp.maximum(jnp.maximum(pre_top, jnp.max(tail_scores, axis=-1)), jnp.max(...]
    add x2 -> x0, other arithmetic: 2.88 us -> none  [per_device(): prefix_total[:, step_index] * shrink + jnp.sum(tail_weights, axis=-1)]
where the time goes in v1:
time: 180 us; the launch traced here: 179 us
  waiting for transfers between devices  119 us (66%)
  Pallas kernels  26.6 us (15%)
  between operations  14.2 us (8%)
  matrix products  8.33 us (5%)
  local copies, waits for them, and re-layouts  7.71 us (4%)
  other arithmetic  3.41 us (2%)
    all_gather x1, waiting for transfers between devices, per_device(): lax.all_gather(stacked, 'prompt', axis=1, tiled=True)  76.2 us
    reduce_scatter x1, waiting for transfers between devices, per_device(): lax.psum_scatter(partial_out.astype(jnp.bfloat16), 'head', scatter_dimens...  42.9 us
    pallas_call x1, Pallas kernels, per_device(): pl.pallas_call(functools.partial(attention_kernel, steps, group), out_sha...  26.6 us
    dot_general x1, matrix products, per_device(): jnp.dot(lax.all_gather(stacked, 'prompt', axis=1, tiled=True), out_weight...  8.33 us
    unnamed x16, local copies, waits for them, and re-layouts  7.62 us
  transfers between devices with their start and end apart: 2, of which 2 were waited for; matrix products, arithmetic and copies ran while one was open for 0% of the time, Pallas kernels for 0%

profile of v1, /device:TPU:0, one launch (start us, length us, event | category | flops | bytes accessed | tf_op | source)
XLA Modules:
  0.0 179.4 jit_solution(11325276896149417039)
XLA Ops:
  6.5 0.0 copy-start
  6.5 0.0 all-gather.2.cloned.1.call-start
  7.4 0.7 fusion.2
  8.1 0.1 select_n.20.bias_ref
  8.2 2.7 %fusion.1.live_ref = f32[2048,128]{1,0:T(8,128)} fusion(s32[]{:T(128)} %bitcast.13, s32[2048]{0:T(1024)S(1)} %get-tuple-element.5, s32[2048]{0:T(1024)S(1)} %get-tuple-element.6, pred[2048]{0:T(1024)(128)(4,1)S(1)} %fusion.5), kind=kLoop, calls=%fused_computation.3 | loop fusion | flops 786432 | bytes 1067012 | tf_op jit(solution)/shard_map/convert_element_type | solution.py:117
  10.8 0.0 copy-start.1
  10.8 1.2 copy-done.1
  12.1 0.0 copy-start.2
  12.1 1.2 copy-done.2
  13.3 0.0 copy-start.3
  13.3 1.2 copy-done.3
  14.5 0.0 copy-start.4
  14.5 1.2 copy-done.4
  15.7 1.0 copy-done.5
  16.8 0.8 copy-done.6
  17.6 0.8 copy-done.7
  18.5 26.6 %shard_map.100 = bf16[4,64,1024]{2,1,0:T(8,128)(2,1)} custom-call(bf16[2048,128]{1,0:T(8,128)(2,1)S(1)} %bitcast.18, bf16[4096,128]{1,0:T(8,128)(2,1)S(1)} %bitcast.14, bf16[4096,128]{1,0:T(8,128)(2,1)S(1)} %bitcast.15, bf16[4096,128]{1,0:T(8,128)(2,1)S(1)} %bitcast.16, bf16[4096,128]{1,0:T(8,128)(2,1)S(1)} %bitcast.17, bf16[256,128]{1,0:T(8,128)(2,1)S(1)} %bitcast.19, ...), custom_call_target="tpu_custom_call" | custom-call | tf_op jit(solution)/shard_map/pallas_call | solution.py:134
  45.0 0.0 all-gather.2.cloned.1.call-update
  45.1 0.0 reduce-scatter.2.cloned.1.call-start
  45.1 76.2 %all-gather.2.cloned.1.call-done = bf16[4,512,1024]{2,1,0:T(8,128)(2,1)} async-done(((bf16[4,64,1024]{2,1,0:T(8,128)(2,1)}), bf16[4,512,1024]{2,1,0:T(8,128)(2,1)}) %all-gather.2.cloned.1.call-update) | async-done | bytes 4194320 | tf_op jit(solution)/shard_map/all_gather | solution.py:147
  121.3 0.0 copy-done
  121.3 8.3 %convolution_convert_fusion = bf16[4,512,1024]{2,1,0:T(8,128)(2,1)} fusion(bf16[4,512,1024]{2,1,0:T(8,128)(2,1)} %all-gather.2.cloned.1.call-done, bf16[1024,1024]{1,0:T(8,128)(2,1)S(1)} %copy-done), kind=kOutput, calls=%fused_computation | convolution fusion | flops 4297064448 | bytes 10485760 | tf_op jit(solution)/shard_map/dot_general | solution.py:146
  129.6 0.0 reduce-scatter.2.cloned.1.call-update
  129.6 42.9 %reduce-scatter.2.cloned.1.call-done = bf16[4,128,1024]{2,1,0:T(8,128)(2,1)} async-done(((bf16[4,512,1024]{2,1,0:T(8,128)(2,1)}), bf16[4,128,1024]{2,1,0:T(8,128)(2,1)}) %reduce-scatter.2.cloned.1.call-update) | async-done | bytes 1048592 | tf_op jit(solution)/shard_map/reduce_scatter | solution.py:149
  (5 shorter events, 0.0 us)
Async XLA Ops:
  6.5 114.8 %copy-start = (bf16[1024,1024]{1,0:T(8,128)(2,1)S(1)}, bf16[1024,1024]{1,0:T(8,128)(2,1)}, u32[]{:S(2)}) copy-start(bf16[1024,1024]{1,0:T(8,128)(2,1)} %param.19) | copy-start | bytes 6291460
  6.5 114.8 %all-gather.2.cloned.1.call-start = ((), (), s32[]{:S(2)}) async-start(), calls=%async_computation.1 | async-start | bytes 4718592 | tf_op jit(solution)/shard_map/all_gather | solution.py:147
  10.8 1.2 copy-start.1
  12.1 1.2 copy-start.2
  13.3 1.2 copy-start.3
  14.5 1.2 copy-start.4
  15.7 1.0 copy-start.5
  16.8 0.8 copy-start.6
  17.6 0.8 copy-start.7
  45.1 127.5 %reduce-scatter.2.cloned.1.call-start = ((), (), s32[]{:S(2)}) async-start(), calls=%async_computation.2 | async-start | bytes 5242880 | tf_op jit(solution)/shard_map/reduce_scatter | solution.py:149
Sparse Core Ops, SparseCore 0:
  45.2 76.0 all-gather.1
  129.8 42.7 reduce-scatter.1

commit v2 on v1

--- a/solution.py
+++ b/solution.py
@@ -14,7 +14,7 @@
 
 
 def attend_chunk(
-    first, q_ref, key_ref, val_ref, tk_ref, tv_ref, nk_ref, nv_ref, bias_ref, live_ref,
+    first, q_ref, key_ref, val_ref, tk_ref, tv_ref, nk_ref, nv_ref, bias_ref, count_ref,
     score_ref, mixed_ref, steps, group,
 ):
     hd = q_ref.shape[1]
@@ -73,8 +73,8 @@
     numer = numer + wide[:, :hd]
     total = total + wide[:, hd:hd + 1]
     mixed = numer / total
-    live = live_ref[pl.ds(pl.multiple_of(first * per, rows), rows), :]
-    mixed_ref[...] = jnp.where(live > 0.0, mixed, 0.0)
+    sample = first + lax.broadcasted_iota(jnp.int32, mixed.shape, 0) // per
+    mixed_ref[...] = jnp.where(sample < count_ref[0], mixed, 0.0)
 
 
 def place_chunk(mixed_ref, out_ref, row, first, steps, group, hd):
@@ -91,7 +91,7 @@
 
 
 def attention_kernel(
-    steps, group, q_ref, k_ref, v_ref, tk_ref, tv_ref, nk_ref, nv_ref, bias_ref, live_ref, out_ref,
+    steps, group, q_ref, k_ref, v_ref, tk_ref, tv_ref, nk_ref, nv_ref, bias_ref, count_ref, out_ref,
     val_ref, score_ref, mixed_ref,
 ):
     hd = q_ref.shape[1]
@@ -100,7 +100,7 @@
 
     def body(c, _):
         first = c * SAMPLES
-        attend_chunk(first, q_ref, k_ref, val_ref, tk_ref, tv_ref, nk_ref, nv_ref, bias_ref, live_ref,
+        attend_chunk(first, q_ref, k_ref, val_ref, tk_ref, tv_ref, nk_ref, nv_ref, bias_ref, count_ref,
                      score_ref, mixed_ref, steps, group)
         place_chunk(mixed_ref, out_ref, 0, first, steps, group, hd)
         return 0
@@ -113,20 +113,156 @@
     suffix = suffix_keys.shape[3]
     bias = jnp.where(lax.broadcasted_iota(jnp.int32, (slots, suffix), 1) < suffix_lengths[0][:, None], 0.0, NEG)
     bias = bias.astype(jnp.float32).reshape(1, slots * suffix)
-    per = steps * group
-    live = (lax.broadcasted_iota(jnp.int32, (slots * per, hd), 0) // per < sample_counts[0]).astype(jnp.float32)
     return (
-        queries.reshape(slots * per, hd),
+        queries.reshape(slots * steps * group, hd),
         prefix_keys[0, 0], prefix_values[0, 0],
         suffix_keys.reshape(slots * suffix, hd), suffix_values.reshape(slots * suffix, hd),
         new_keys.reshape(slots * steps, hd), new_values.reshape(slots * steps, hd),
-        bias, live,
+        bias, sample_counts,
     )
+
+
+def project_kernel(
+    ring, heads, x_ref, w_ref, out_ref, held, sent, own, landed,
+    hop_send, hop_recv, sum_send, sum_recv,
+):
+    steps, slots, depth = x_ref.shape
+    half = steps // 2
+    share = ring // heads
+    cols = w_ref.shape[1]
+    me = lax.axis_index("prompt")
+    head = lax.axis_index("head")
+    mesh_id = pl.DeviceIdType.MESH
+
+    def prompt_at(spot):
+        spot = lax.rem(spot + 2 * ring, ring)
+        return jnp.where(spot < ring // 2, 2 * spot, 2 * (ring - 1 - spot) + 1)
+
+    spot = jnp.where(lax.rem(me, 2) == 0, me // 2, ring - 1 - me // 2)
+    right, left = prompt_at(spot + 1), prompt_at(spot - 1)
+
+    barrier = pltpu.get_barrier_semaphore()
+    for other in (left, right):
+        pl.semaphore_signal(barrier, inc=1, device_id=(other, head), device_id_type=mesh_id)
+    for d in range(1, heads):
+        pl.semaphore_signal(barrier, inc=1, device_id=(me, lax.rem(head + d, heads)), device_id_type=mesh_id)
+    pl.semaphore_wait(barrier, 1 + heads)
+
+    def hop(k, t):
+        return pltpu.make_async_remote_copy(
+            src_ref=held.at[k - 1, t], dst_ref=held.at[k, t],
+            send_sem=hop_send.at[k - 1, t], recv_sem=hop_recv.at[k - 1, t],
+            device_id=(right if t < half else left, head), device_id_type=mesh_id,
+        )
+
+    def spread(k, side, source, target, prompt):
+        at = lax.rem(prompt, share)
+        return pltpu.make_async_remote_copy(
+            src_ref=sent.at[k, side],
+            dst_ref=landed.at[source, at, side],
+            send_sem=sum_send.at[k, side], recv_sem=sum_recv.at[source, at, side],
+            device_id=(me, target), device_id_type=mesh_id,
+        )
+
+    def prompt_of(k, side):
+        return prompt_at(spot - k if side == 0 else spot + k)
+
+    held[0] = x_ref[...]
+    for t in range(steps):
+        hop(1, t).start()
+
+    def step(k, _):
+        @pl.when(k > 0)
+        def _():
+            for t in (0, half, 1, half + 1) if steps == 4 else range(steps):
+                hop(k, t).wait_recv()
+
+                @pl.when(k < ring - 1)
+                def _():
+                    hop(k + 1, t).start()
+
+        block = held[k].reshape(steps * slots, depth)
+        y = jnp.dot(block, w_ref[...], preferred_element_type=jnp.float32)
+        for side in range(2):
+            prompt = prompt_of(k, side)
+            target = prompt // share
+            rows = y[side * half * slots:(side + 1) * half * slots].reshape(half, slots, cols)
+
+            @pl.when(target == head)
+            def _():
+                own[lax.rem(prompt, share), side] = rows
+
+            @pl.when(target != head)
+            def _():
+                sent[k, side] = rows.astype(jnp.bfloat16)
+                spread(k, side, head, target, prompt).start()
+        return 0
+
+    lax.fori_loop(0, ring, step, 0)
+
+    def drain(k, _):
+        for side in range(2):
+            prompt = prompt_of(k, side)
+            target = prompt // share
+
+            @pl.when(target != head)
+            def _():
+                spread(k, side, head, target, prompt).wait_send()
+
+        @pl.when(k > 0)
+        def _():
+            for t in range(steps):
+                hop(k, t).wait_send()
+        return 0
+
+    def finish(at, _):
+        for side in range(2):
+            for d in range(1, heads):
+                source = lax.rem(head + d, heads)
+                pltpu.make_async_remote_copy(
+                    src_ref=sent.at[0, side], dst_ref=landed.at[source, at, side],
+                    send_sem=sum_send.at[0, side], recv_sem=sum_recv.at[source, at, side],
+                    device_id=(me, source), device_id_type=mesh_id,
+                ).wait_recv()
+            for t in range(half):
+                total = own[at, side, t]
+                for d in range(1, heads):
+                    total = total + landed[lax.rem(head + d, heads), at, side, t].astype(jnp.float32)
+                out_ref[side * half + t, pl.ds(pl.multiple_of(at * slots, slots), slots), :] = total.astype(out_ref.dtype)
+        return 0
+
+    lax.fori_loop(0, share, finish, 0)
+    lax.fori_loop(0, ring, drain, 0)
+
+
+def project(stacked, out_weight, ring, heads):
+    steps, slots, depth = stacked.shape
+    cols = out_weight.shape[1]
+    half, share = steps // 2, ring // heads
+    return pl.pallas_call(
+        functools.partial(project_kernel, ring, heads),
+        out_shape=jax.ShapeDtypeStruct((steps, share * slots, cols), jnp.bfloat16),
+        in_specs=[pl.BlockSpec(memory_space=pltpu.VMEM)] * 2,
+        out_specs=pl.BlockSpec(memory_space=pltpu.VMEM),
+        scratch_shapes=[
+            pltpu.VMEM((ring, steps, slots, depth), jnp.bfloat16),
+            pltpu.VMEM((ring, 2, half, slots, cols), jnp.bfloat16),
+            pltpu.VMEM((share, 2, half, slots, cols), jnp.float32),
+            pltpu.VMEM((heads, share, 2, half, slots, cols), jnp.bfloat16),
+            pltpu.SemaphoreType.DMA((ring, steps)),
+            pltpu.SemaphoreType.DMA((ring, steps)),
+            pltpu.SemaphoreType.DMA((ring, 2)),
+            pltpu.SemaphoreType.DMA((heads, share, 2)),
+        ],
+        compiler_params=pltpu.CompilerParams(
+            collective_id=0, has_side_effects=True, vmem_limit_bytes=48 * 2**20
+        ),
+    )(stacked, out_weight)
 
 
 def per_device(
     queries, new_keys, new_values, prefix_keys, prefix_values, suffix_keys, suffix_values,
-    suffix_lengths, sample_counts, out_weight,
+    suffix_lengths, sample_counts, out_weight, *, ring, heads,
 ):
     _, slots, steps, group, hd = queries.shape
     ins = prepare(queries, new_keys, new_values, prefix_keys, prefix_values, suffix_keys, suffix_values, suffix_lengths, sample_counts)
@@ -134,7 +270,7 @@
     stacked = pl.pallas_call(
         functools.partial(attention_kernel, steps, group),
         out_shape=jax.ShapeDtypeStruct((steps, slots, group * hd), jnp.bfloat16),
-        in_specs=[pl.BlockSpec(memory_space=pltpu.VMEM)] * 9,
+        in_specs=[pl.BlockSpec(memory_space=pltpu.VMEM)] * 8 + [pl.BlockSpec(memory_space=pltpu.SMEM)],
         out_specs=pl.BlockSpec(memory_space=pltpu.VMEM),
         scratch_shapes=[
             pltpu.VMEM((prefix, 2 * hd), jnp.bfloat16),
@@ -143,15 +279,13 @@
         ],
         compiler_params=pltpu.CompilerParams(vmem_limit_bytes=48 * 2**20),
     )(*ins)
-    partial_out = jnp.dot(
-        lax.all_gather(stacked, "prompt", axis=1, tiled=True), out_weight, preferred_element_type=jnp.float32
-    )
-    return lax.psum_scatter(partial_out.astype(jnp.bfloat16), "head", scatter_dimension=1, tiled=True)
+    return project(stacked, out_weight, ring, heads)
 
 
 def solution(mesh):
+    ring, heads = mesh.shape["prompt"], mesh.shape["head"]
     return jax.shard_map(
-        per_device,
+        functools.partial(per_device, ring=ring, heads=heads),
         mesh=mesh,
         in_specs=(
             P("prompt", None, None, "head", None),

time: 180 us -> 98.4 us (0.55)
  waiting for transfers between devices: 119 us -> 0 us
  Pallas kernels: 26.6 us -> 87.6 us
  between operations: 14.2 us -> 0.7 us
  matrix products: 8.33 us -> 0 us
  other arithmetic: 3.41 us -> 0.73 us
    all_gather x1 -> x0, waiting for transfers between devices: 76.2 us -> none  [per_device(): lax.all_gather(stacked, 'prompt', axis=1, tiled=True)]
    pallas_call x0 -> x1, Pallas kernels: none -> 63 us  [project(): pl.pallas_call(functools.partial(project_kernel, ring, heads), out_shape=...]
    reduce_scatter x1 -> x0, waiting for transfers between devices: 42.9 us -> none  [per_device(): lax.psum_scatter(partial_out.astype(jnp.bfloat16), 'head', scatter_dimens...]
    dot_general x1 -> x0, matrix products: 8.33 us -> none  [per_device(): jnp.dot(lax.all_gather(stacked, 'prompt', axis=1, tiled=True), out_weight...]
    convert_element_type x1 -> x0, other arithmetic: 2.67 us -> none  [prepare(): (lax.broadcasted_iota(jnp.int32, (slots * per, hd), 0) // per < sample_co...]
    pallas_call x1, Pallas kernels: 26.6 us -> 24.6 us  [per_device(): pl.pallas_call(functools.partial(attention_kernel, steps, group), out_sha...]
    unnamed x16 -> x17, local copies, waits for them, and re-layouts: 7.62 us -> 8.59 us
  transfers between devices with their start and end apart: 2 -> 0, of which waited for: 2 -> 0; matrix products, arithmetic and copies ran while one was open for 0% -> 0% of each run, Pallas kernels for 0% -> 0%
where the time goes in v2:
time: 98.4 us; the launch traced here: 97.7 us
  Pallas kernels  87.6 us (89%)
  local copies, waits for them, and re-layouts  8.68 us (9%)
    pallas_call x1, Pallas kernels, project(): pl.pallas_call(functools.partial(project_kernel, ring, heads), out_shape=...  63 us
    pallas_call x1, Pallas kernels, per_device(): pl.pallas_call(functools.partial(attention_kernel, steps, group), out_sha...  24.6 us
    unnamed x17, local copies, waits for them, and re-layouts  8.59 us

profile of v2, /device:TPU:0, one launch (start us, length us, event | category | flops | bytes accessed | tf_op | source)
XLA Modules:
  0.0 97.7 jit_solution(11063868891702058331)
XLA Ops:
  0.7 0.7 fusion
  1.4 0.1 select_n.15.bias_ref
  1.5 0.0 copy-start.1
  1.5 1.2 %copy-done.1 = bf16[1,1,4096,128]{3,2,1,0:T(8,128)(2,1)S(1)} copy-done((bf16[1,1,4096,128]{3,2,1,0:T(8,128)(2,1)S(1)}, bf16[1,1,4096,128]{3,2,1,0:T(8,128)(2,1)}, u32[]{:S(2)}) %copy-start.1) | copy-done | bytes 1048600
  2.7 0.0 copy-start.2
  2.7 1.2 %copy-done.2 = bf16[1,1,4096,128]{3,2,1,0:T(8,128)(2,1)S(1)} copy-done((bf16[1,1,4096,128]{3,2,1,0:T(8,128)(2,1)S(1)}, bf16[1,1,4096,128]{3,2,1,0:T(8,128)(2,1)}, u32[]{:S(2)}) %copy-start.2) | copy-done | bytes 1048600
  3.9 0.0 copy-start.3
  3.9 1.2 %copy-done.3 = bf16[1,64,1,64,128]{4,3,2,1,0:T(8,128)(2,1)S(1)} copy-done((bf16[1,64,1,64,128]{4,3,2,1,0:T(8,128)(2,1)S(1)}, bf16[1,64,1,64,128]{4,3,2,1,0:T(8,128)(2,1)}, u32[]{:S(2)}) %copy-start.3) | copy-done | bytes 1048600
  5.2 0.0 copy-start.4
  5.2 1.2 %copy-done.4 = bf16[1,64,1,64,128]{4,3,2,1,0:T(8,128)(2,1)S(1)} copy-done((bf16[1,64,1,64,128]{4,3,2,1,0:T(8,128)(2,1)S(1)}, bf16[1,64,1,64,128]{4,3,2,1,0:T(8,128)(2,1)}, u32[]{:S(2)}) %copy-start.4) | copy-done | bytes 1048600
  6.4 0.0 copy-start.5
  6.4 1.0 %copy-done.5 = bf16[1,64,4,8,128]{4,3,2,1,0:T(8,128)(2,1)S(1)} copy-done((bf16[1,64,4,8,128]{4,3,2,1,0:T(8,128)(2,1)S(1)}, bf16[1,64,4,8,128]{4,3,2,1,0:T(8,128)(2,1)}, u32[]{:S(2)}) %copy-start.5) | copy-done | bytes 524312
  7.4 0.0 copy-start.6
  7.4 0.8 copy-done.6
  8.3 0.0 copy-start.7
  8.3 0.8 copy-done.7
  9.1 0.0 copy-start
  9.1 24.6 %shard_map.100.x_ref = bf16[4,64,1024]{2,1,0:T(8,128)(2,1)S(1)} custom-call(bf16[2048,128]{1,0:T(8,128)(2,1)S(1)} %bitcast.12, bf16[4096,128]{1,0:T(8,128)(2,1)S(1)} %bitcast.8, bf16[4096,128]{1,0:T(8,128)(2,1)S(1)} %bitcast.9, bf16[4096,128]{1,0:T(8,128)(2,1)S(1)} %bitcast.10, bf16[4096,128]{1,0:T(8,128)(2,1)S(1)} %bitcast.11, ...), custom_call_target="tpu_custom_call" | custom-call | tf_op jit(solution)/shard_map/pallas_call | solution.py:270
  33.7 0.0 copy-done
  33.7 63.0 %shard_map.101 = bf16[4,128,1024]{2,1,0:T(8,128)(2,1)S(1)} custom-call(bf16[4,64,1024]{2,1,0:T(8,128)(2,1)S(1)} %shard_map.100.x_ref, bf16[1024,1024]{1,0:T(8,128)(2,1)S(1)} %copy-done), custom_call_target="tpu_custom_call" | custom-call | tf_op jit(solution)/shard_map/pallas_call | solution.py:242
  96.7 1.0 copy.13
Async XLA Ops:
  1.5 1.2 %copy-start.1 = (bf16[1,1,4096,128]{3,2,1,0:T(8,128)(2,1)S(1)}, bf16[1,1,4096,128]{3,2,1,0:T(8,128)(2,1)}, u32[]{:S(2)}) copy-start(bf16[1,1,4096,128]{3,2,1,0:T(8,128)(2,1)} %param.13) | copy-start | bytes 3145732
  2.7 1.2 %copy-start.2 = (bf16[1,1,4096,128]{3,2,1,0:T(8,128)(2,1)S(1)}, bf16[1,1,4096,128]{3,2,1,0:T(8,128)(2,1)}, u32[]{:S(2)}) copy-start(bf16[1,1,4096,128]{3,2,1,0:T(8,128)(2,1)} %param.14) | copy-start | bytes 3145732
  3.9 1.2 %copy-start.3 = (bf16[1,64,1,64,128]{4,3,2,1,0:T(8,128)(2,1)S(1)}, bf16[1,64,1,64,128]{4,3,2,1,0:T(8,128)(2,1)}, u32[]{:S(2)}) copy-start(bf16[1,64,1,64,128]{4,3,2,1,0:T(8,128)(2,1)} %param.15) | copy-start | bytes 3145732
  5.2 1.2 %copy-start.4 = (bf16[1,64,1,64,128]{4,3,2,1,0:T(8,128)(2,1)S(1)}, bf16[1,64,1,64,128]{4,3,2,1,0:T(8,128)(2,1)}, u32[]{:S(2)}) copy-start(bf16[1,64,1,64,128]{4,3,2,1,0:T(8,128)(2,1)} %param.16) | copy-start | bytes 3145732
  6.4 1.0 %copy-start.5 = (bf16[1,64,4,8,128]{4,3,2,1,0:T(8,128)(2,1)S(1)}, bf16[1,64,4,8,128]{4,3,2,1,0:T(8,128)(2,1)}, u32[]{:S(2)}) copy-start(bf16[1,64,4,8,128]{4,3,2,1,0:T(8,128)(2,1)} %param.10) | copy-start | bytes 1572868
  7.4 0.8 copy-start.6
  8.3 0.8 copy-start.7
  9.1 24.6 %copy-start = (bf16[1024,1024]{1,0:T(8,128)(2,1)S(1)}, bf16[1024,1024]{1,0:T(8,128)(2,1)}, u32[]{:S(2)}) copy-start(bf16[1024,1024]{1,0:T(8,128)(2,1)} %w_ref.1) | copy-start | bytes 6291460

commit v3 on v1

v3 whole, which is shorter than its diff:
```python
import functools
import math

import jax
import jax.numpy as jnp
from jax import lax
from jax.experimental import pallas as pl
from jax.experimental.pallas import tpu as pltpu
from jax.sharding import PartitionSpec as P

NEG = -1e30
SAMPLES = 16
GROUPED = 4


def attend_chunk(
    first, q_ref, key_ref, val_ref, tk_ref, tv_ref, nk_ref, nv_ref, bias_ref, count_ref,
    score_ref, mixed_ref, steps, group, midway,
):
    hd = q_ref.shape[1]
    per = steps * group
    rows = SAMPLES * per
    suffix = tk_ref.shape[0] * per // q_ref.shape[0]
    scale = (hd ** -0.5) * math.log2(math.e)
    nt = (((1,), (1,)), ((), ()))
    f32 = jnp.float32
    prefix = key_ref.shape[0]
    tile = 512
    sub = GROUPED * per
    q = q_ref[pl.ds(pl.multiple_of(first * per, rows), rows), :]
    top = None
    for k in range(prefix // tile):
        s = lax.dot_general(q, key_ref[k * tile:(k + 1) * tile, :], nt, preferred_element_type=f32)
        score_ref[:, k * tile:(k + 1) * tile] = s
        for c in range(tile // 128):
            piece = s[:, c * 128:(c + 1) * 128]
            top = piece if top is None else jnp.maximum(top, piece)
    row_top = jnp.max(top, axis=1, keepdims=True)
    nk = nk_ref[pl.ds(pl.multiple_of(first * steps, SAMPLES * steps), SAMPLES * steps), :]
    nv = nv_ref[pl.ds(pl.multiple_of(first * steps, SAMPLES * steps), SAMPLES * steps), :]
    ns = lax.dot_general(q, nk, nt, preferred_element_type=f32)
    r = lax.broadcasted_iota(jnp.int32, ns.shape, 0)
    j = lax.broadcasted_iota(jnp.int32, ns.shape, 1)
    ok = (j // steps == r // per) & (j % steps <= (r % per) // group)
    ns = jnp.where(ok, ns, NEG)
    row_top = jnp.maximum(row_top, jnp.max(ns, axis=1, keepdims=True))
    width = GROUPED * suffix
    tails = []
    for g in range(SAMPLES // GROUPED):
        at = pl.multiple_of((first + g * GROUPED) * suffix, width)
        ts = lax.dot_general(q[g * sub:(g + 1) * sub], tk_ref[pl.ds(at, width), :], nt, preferred_element_type=f32)
        r = lax.broadcasted_iota(jnp.int32, ts.shape, 0)
        j = lax.broadcasted_iota(jnp.int32, ts.shape, 1)
        ts = jnp.where(j // suffix == r // per, ts + bias_ref[:, pl.ds(at, width)], NEG)
        tails.append(ts)
    tail = jnp.concatenate(tails, axis=0)
    row_top = jnp.maximum(row_top, jnp.max(tail, axis=1, keepdims=True))
    midway()
    nw = jnp.exp2((ns - row_top) * scale)
    tw = jnp.exp2((tail - row_top) * scale)
    total = jnp.sum(nw, axis=1, keepdims=True) + jnp.sum(tw, axis=1, keepdims=True)
    numer = jnp.dot(nw.astype(jnp.bfloat16), nv, preferred_element_type=f32)
    tw = tw.astype(jnp.bfloat16)
    parts = []
    for g in range(SAMPLES // GROUPED):
        at = pl.multiple_of((first + g * GROUPED) * suffix, width)
        parts.append(jnp.dot(tw[g * sub:(g + 1) * sub], tv_ref[pl.ds(at, width), :], preferred_element_type=f32))
    numer = numer + jnp.concatenate(parts, axis=0)
    wide = None
    for k in range(prefix // tile):
        w = jnp.exp2((score_ref[:, k * tile:(k + 1) * tile] - row_top) * scale).astype(jnp.bfloat16)
        d = jnp.dot(w, val_ref[k * tile:(k + 1) * tile, :], preferred_element_type=f32)
        wide = d if wide is None else wide + d
    numer = numer + wide[:, :hd]
    total = total + wide[:, hd:hd + 1]
    mixed = numer / total
    sample = first + lax.broadcasted_iota(jnp.int32, mixed.shape, 0) // per
    mixed_ref[...] = jnp.where(sample < count_ref[0], mixed, 0.0)


def place_chunk(mixed_ref, held, c, steps, group, hd):
    half = steps // 2
    for t in range(steps):
        for g in range(group):
            piece = mixed_ref[pl.ds(t * group + g, SAMPLES, stride=steps * group), :]
            held[0, t // half, c, t % half, :, g * hd:(g + 1) * hd] = piece.astype(jnp.bfloat16)


def layer_kernel(
    ring, heads, steps, group,
    q_hbm, k_hbm, v_hbm, tk_hbm, tv_hbm, w_hbm, nk_ref, nv_ref, bias_ref, count_ref, out_ref,
    q_ref, k_ref, val_ref, tk_ref, tv_ref, w_ref, score_ref, mixed_ref,
    held, keep, sent, paired, own, landed,
    in_sem, hop_send, hop_recv, sum_send, pair_recv, sum_recv,
):
    hd = q_ref.shape[1]
    chunks = held.shape[2]
    half = steps // 2
    side_rows = chunks * half * SAMPLES
    depth = held.shape[-1]
    share = ring // heads
    chips = heads // 2
    last = 2 * chunks - 1
    me = lax.axis_index("prompt")
    head = lax.axis_index("head")
    chip, core = head // 2, lax.rem(head, 2)
    sibling = 2 * chip + 1 - core
    mesh_id = pl.DeviceIdType.MESH

    val_ref[:, hd:] = jnp.ones((val_ref.shape[0], hd), val_ref.dtype)
    loads = [
        pltpu.make_async_copy(src, dst, in_sem.at[i])
        for i, (src, dst) in enumerate((
            (q_hbm, q_ref), (k_hbm, k_ref), (v_hbm, val_ref.at[:, pl.ds(0, hd)]),
            (tk_hbm, tk_ref), (tv_hbm, tv_ref), (w_hbm, w_ref),
        ))
    ]
    for load in loads:
        load.start()

    def prompt_at(spot):
        spot = lax.rem(spot + 2 * ring, ring)
        return jnp.where(spot < ring // 2, 2 * spot, 2 * (ring - 1 - spot) + 1)

    spot = jnp.where(lax.rem(me, 2) == 0, me // 2, ring - 1 - me // 2)
    right, left = prompt_at(spot + 1), prompt_at(spot - 1)

    barrier = pltpu.get_barrier_semaphore()
    for other in (left, right):
        pl.semaphore_signal(barrier, inc=1, device_id=(other, head), device_id_type=mesh_id)
    pl.semaphore_signal(barrier, inc=1, device_id=(me, sibling), device_id_type=mesh_id)
    for d in range(1, chips):
        pl.semaphore_signal(
            barrier, inc=1, device_id=(me, lax.rem(head + 2 * d, heads)), device_id_type=mesh_id
        )
    pl.semaphore_wait(barrier, 2 + chips)

    def hop(k, side, c):
        return pltpu.make_async_remote_copy(
            src_ref=held.at[k - 1, side, c], dst_ref=held.at[k, side, c],
            send_sem=hop_send.at[k - 1, side, c], recv_sem=hop_recv.at[k - 1, side, c],
            device_id=(left if side else right, head), device_id_type=mesh_id,
        )

    def pass_on(c, late):
        for older in range(chunks - 1):
            k = 2 * (c - older) - 1 + late

            @pl.when((older < c) & (k < ring - 1))
            def _():
                for side in range(2):
                    hop(k, side, older).wait_recv()
                    hop(k + 1, side, older).start()

    for load in loads[:5]:
        load.wait()

    def attend(c, _):
        attend_chunk(
            c * SAMPLES, q_ref, k_ref, val_ref, tk_ref, tv_ref, nk_ref, nv_ref, bias_ref, count_ref,
            score_ref, mixed_ref, steps, group, lambda: pass_on(c, 0),
        )
        place_chunk(mixed_ref, held, c, steps, group, hd)
        for side in range(2):
            hop(1, side, c).start()
        pass_on(c, 1)
        return 0

    lax.fori_loop(0, chunks, attend, 0)
    loads[5].wait()

    def prompt_of(k, side):
        return prompt_at(spot - k if side == 0 else spot + k)

    def to_sibling(k, side):
        return pltpu.make_async_remote_copy(
            src_ref=sent.at[k, side], dst_ref=paired.at[k, side],
            send_sem=sum_send.at[k, side], recv_sem=pair_recv.at[k, side],
            device_id=(me, sibling), device_id_type=mesh_id,
        )

    def to_holder(k, side, source, at, target):
        return pltpu.make_async_remote_copy(
            src_ref=sent.at[k, side], dst_ref=landed.at[source, at, side],
            send_sem=sum_send.at[k, side], recv_sem=sum_recv.at[source, at, side],
            device_id=(me, target), device_id_type=mesh_id,
        )

    def step(k, _):
        @pl.when(k < ring)
        def _():
            for c in range(chunks):
                @pl.when((k > 0) & ((k > last - 2 * c - 1) | (k == ring - 1)))
                def _():
                    for side in range(2):
                        hop(k, side, c).wait_recv()

                        @pl.when(k < ring - 1)
                        def _():
                            hop(k + 1, side, c).start()

            block = held[k].reshape(2 * side_rows, depth)
            y = jnp.dot(block, w_ref[...], preferred_element_type=jnp.float32)
            for side in range(2):
                target = prompt_of(k, side) // share
                rows = y[side * side_rows:(side + 1) * side_rows]

                @pl.when(lax.rem(target, 2) == core)
                def _():
                    keep[k, side] = rows

                @pl.when(lax.rem(target, 2) != core)
                def _():
                    sent[k, side] = rows.astype(jnp.bfloat16)
                    to_sibling(k, side).start()

        @pl.when(k > 0)
        def _():
            for side in range(2):
                prompt = prompt_of(k - 1, side)
                target = prompt // share
                at = lax.rem(prompt, share)

                @pl.when(lax.rem(target, 2) == core)
                def _():
                    to_sibling(k - 1, side).wait_recv()
                    both = keep[k - 1, side] + paired[k - 1, side].astype(jnp.float32)

                    @pl.when(target == head)
                    def _():
                        own[at, side] = both

                    @pl.when(target != head)
                    def _():
                        sent[k - 1, side] = both.astype(jnp.bfloat16)
                        to_holder(k - 1, side, chip, at, target).start()
        return 0

    lax.fori_loop(0, ring + 1, step, 0)

    def finish(at, _):
        for side in range(2):
            for d in range(1, chips):
                source = lax.rem(chip + d, chips)
                to_holder(0, side, source, at, 2 * source + core).wait_recv()
            total = own[at, side]
            for d in range(1, chips):
                total = total + landed[lax.rem(chip + d, chips), at, side].astype(jnp.float32)
            total = total.astype(out_ref.dtype)
            for c in range(chunks):
                for t in range(half):
                    row = (c * half + t) * SAMPLES
                    to = pl.multiple_of((at * chunks + c) * SAMPLES, SAMPLES)
                    out_ref[side * half + t, pl.ds(to, SAMPLES), :] = total[row:row + SAMPLES]
        return 0

    lax.fori_loop(0, share, finish, 0)

    def drain(k, _):
        for side in range(2):
            @pl.when(prompt_of(k, side) // share != head)
            def _():
                to_sibling(k, side).wait_send()

            @pl.when(k > 0)
            def _():
                for c in range(chunks):
                    hop(k, side, c).wait_send()
        return 0

    lax.fori_loop(0, ring, drain, 0)


def per_device(
    queries, new_keys, new_values, prefix_keys, prefix_values, suffix_keys, suffix_values,
    suffix_lengths, sample_counts, out_weight, *, ring, heads,
):
    _, slots, steps, group, hd = queries.shape
    suffix = suffix_keys.shape[3]
    prefix = prefix_keys.shape[2]
    bias = jnp.where(lax.broadcasted_iota(jnp.int32, (slots, suffix), 1) < suffix_lengths[0][:, None], 0.0, NEG)
    bias = bias.astype(jnp.float32).reshape(1, slots * suffix)
    rows, depth = slots * steps * group, group * hd
    cols = out_weight.shape[1]
    half, share, chips, chunks = steps // 2, ring // heads, heads // 2, slots // SAMPLES
    side = chunks * half * SAMPLES
    hbm = pl.BlockSpec(memory_space=pltpu.HBM)
    vmem = pl.BlockSpec(memory_space=pltpu.VMEM)
    bf16, f32 = jnp.bfloat16, jnp.float32
    dma = pltpu.SemaphoreType.DMA
    return pl.pallas_call(
        functools.partial(layer_kernel, ring, heads, steps, group),
        out_shape=jax.ShapeDtypeStruct((steps, share * slots, cols), bf16),
        in_specs=[hbm] * 6 + [vmem] * 3 + [pl.BlockSpec(memory_space=pltpu.SMEM)],
        out_specs=vmem,
        scratch_shapes=[
            pltpu.VMEM((rows, hd), bf16),
            pltpu.VMEM((prefix, hd), bf16),
            pltpu.VMEM((prefix, 2 * hd), bf16),
            pltpu.VMEM((slots * suffix, hd), bf16),
            pltpu.VMEM((slots * suffix, hd), bf16),
            pltpu.VMEM((depth, cols), bf16),
            pltpu.VMEM((SAMPLES * steps * group, prefix), f32),
            pltpu.VMEM((SAMPLES * steps * group, hd), f32),
            pltpu.VMEM((ring, 2, chunks, half, SAMPLES, depth), bf16),
            pltpu.VMEM((ring, 2, side, cols), f32),
            pltpu.VMEM((ring, 2, side, cols), bf16),
            pltpu.VMEM((ring, 2, side, cols), bf16),
            pltpu.VMEM((share, 2, side, cols), f32),
            pltpu.VMEM((chips, share, 2, side, cols), bf16),
            dma((6,)),
            dma((ring, 2, chunks)),
            dma((ring, 2, chunks)),
            dma((ring, 2)),
            dma((ring, 2)),
            dma((chips, share, 2)),
        ],
        compiler_params=pltpu.CompilerParams(
            collective_id=0, has_side_effects=True, vmem_limit_bytes=58 * 2**20
        ),
    )(
        queries.reshape(rows, hd), prefix_keys[0, 0], prefix_values[0, 0],
        suffix_keys.reshape(slots * suffix, hd), suffix_values.reshape(slots * suffix, hd), out_weight,
        new_keys.reshape(slots * steps, hd), new_values.reshape(slots * steps, hd), bias, sample_counts,
    )


def solution(mesh):
    ring, heads = mesh.shape["prompt"], mesh.shape["head"]
    return jax.shard_map(
        functools.partial(per_device, ring=ring, heads=heads),
        mesh=mesh,
        in_specs=(
            P("prompt", None, None, "head", None),
            P("prompt", None, None, "head", None),
            P("prompt", None, None, "head", None),
            P("prompt", "head", None, None),
            P("prompt", "head", None, None),
            P("prompt", None, "head", None, None),
            P("prompt", None, "head", None, None),
            P("prompt", None),
            P("prompt"),
            P("head", "prompt"),
        ),
        out_specs=P(None, "head", "prompt"),
        check_vma=False,
    )
```

time: 180 us -> 77.5 us (0.43)
  waiting for transfers between devices: 119 us -> 0 us
  Pallas kernels: 26.6 us -> 72.9 us
  between operations: 14.2 us -> 0.66 us
  matrix products: 8.33 us -> 0 us
  local copies, waits for them, and re-layouts: 7.71 us -> 2.96 us
  other arithmetic: 3.41 us -> 0.73 us
    all_gather x1 -> x0, waiting for transfers between devices: 76.2 us -> none  [per_device(): lax.all_gather(stacked, 'prompt', axis=1, tiled=True)]
    pallas_call x1, Pallas kernels: 26.6 us -> 72.9 us  [per_device(): pl.pallas_call(functools.partial(layer_kernel, ring, heads, steps, group)...]
    reduce_scatter x1 -> x0, waiting for transfers between devices: 42.9 us -> none  [per_device(): lax.psum_scatter(partial_out.astype(jnp.bfloat16), 'head', scatter_dimens...]
    dot_general x1 -> x0, matrix products: 8.33 us -> none  [per_device(): jnp.dot(lax.all_gather(stacked, 'prompt', axis=1, tiled=True), out_weight...]
    unnamed x16 -> x1, local copies, waits for them, and re-layouts: 7.62 us -> 2.26 us
    convert_element_type x1 -> x0, other arithmetic: 2.67 us -> none  [prepare(): (lax.broadcasted_iota(jnp.int32, (slots * per, hd), 0) // per < sample_co...]
  transfers between devices with their start and end apart: 2 -> 0, of which waited for: 2 -> 0; matrix products, arithmetic and copies ran while one was open for 0% -> 0% of each run, Pallas kernels for 0% -> 0%
where the time goes in v3:
time: 77.5 us; the launch traced here: 77.3 us
  Pallas kernels  72.9 us (94%)
  local copies, waits for them, and re-layouts  2.96 us (4%)
    pallas_call x1, Pallas kernels, per_device(): pl.pallas_call(functools.partial(layer_kernel, ring, heads, steps, group)...  72.9 us
    unnamed x1, local copies, waits for them, and re-layouts  2.26 us

profile of v3, /device:TPU:0, one launch (start us, length us, event | category | flops | bytes accessed | tf_op | source)
XLA Modules:
  0.0 77.3 jit_solution(4457079586898074967)
XLA Ops:
  0.7 0.7 fusion
  1.4 0.7 select_n.15.bias_ref
  2.1 72.9 %shard_map.100 = bf16[4,128,1024]{2,1,0:T(8,128)(2,1)} custom-call(bf16[2048,128]{1,0:T(8,128)(2,1)} %bitcast.12, bf16[4096,128]{1,0:T(8,128)(2,1)} %bitcast.8, bf16[4096,128]{1,0:T(8,128)(2,1)} %bitcast.9, bf16[4096,128]{1,0:T(8,128)(2,1)} %bitcast.10, bf16[4096,128]{1,0:T(8,128)(2,1)} %bitcast.11, bf16[1024,1024]{1,0:T(8,128)(2,1)} %w_hbm.1, ...), custom_call_target="tpu_custom_call" | custom-call | tf_op jit(solution)/shard_map/pallas_call | solution.py:291
  75.0 2.3 %copy.13 = bf16[4,128,1024]{2,1,0:T(8,128)(2,1)} copy(bf16[4,128,1024]{2,1,0:T(8,128)(2,1)} %shard_map.100) | data formatting | bytes 2097152
